TPU v7x, 256 devices: a whole 4x4x8 slice. The times are simulated.
256 devices in a mesh: row: 16 (over y, x), col: 8 (over z), layer: 2 (over core).
Axes of the slice: x: 4, y: 4, z: 8, core: 2. Of those that a mesh axis runs over, the one named last changes fastest.
Arguments:
- f1_vals: bfloat16 [128, 16, 128, 128], P('row', ('col', 'layer')), may hold values from -6 to 6
- f1_cols: int32 [128, 16], P('row', ('col', 'layer')), may hold values from 0 to 255, as said below
- p0_vals: bfloat16 [256, 16, 128, 128], P(('row', 'layer'), 'col'), may hold values from -0.5 to 0.5
- p0_cols: int32 [256, 16], P(('row', 'layer'), 'col'), may hold values from 0 to 255, as said below
- s_vals: bfloat16 [256, 16, 128, 128], P(('row', 'layer'), 'col'), may hold values from -0.375 to 0.375
- s_cols: int32 [256, 16], P(('row', 'layer'), 'col'), may hold values from 0 to 255, as said below
- p1_filter: int32 [128, 32], P('row', ('col', 'layer')), may hold values from 0 to 255, as said below
- q_filter: int32 [128, 16], P('row', ('col', 'layer')), may hold values from 0 to 255, as said below
Outputs:
- p1_vals: bfloat16 [128, 32, 128, 128], P('row', ('col', 'layer'))
- q_vals: bfloat16 [128, 16, 128, 128], P('row', ('col', 'layer'))
Inputs may be any that keep to these rules, and one draw needn't show every extreme that they name: `f1_cols`: slot g + s of a block row names a block column J of class g, that is J % 8 == g // 2 and (J // 8) % 2 == g % 2; the 1 column of one class in one row are distinct. `p0_cols`: slot u * 2 + w of a block row names a block column J with J % 8 == u; the 2 columns of one u in one row are distinct. `s_cols`: slot u * 2 + w of a block row names a block column J with J % 8 == u; the 2 columns of one u in one row are distinct. `p1_filter`: slot g * 2 + o names a block column of class g as for f1_cols; distinct within a class and row. `q_filter`: slot g + o names a block column of class g as for f1_cols; distinct within a class and row.
All inputs are finite; a program needn't handle non-finite values.
Results may differ from a plain program's by a relative error of at most 0.0085.
Values may be sent and summed in bfloat16 or wider, within the bound.
A program may use at most 128 MiB of HBM per device.

v0:
```python
import jax
import jax.numpy as jnp
from jax import lax
from jax.sharding import PartitionSpec as P


def block_terms(a_values, a_columns, panel, panel_names, wanted, tile_rows, layers):
    panel_rows = a_columns // (tile_rows * layers) * tile_rows + a_columns % tile_rows
    picked = jnp.take(panel, panel_rows, axis=0)
    picked_names = jnp.take(panel_names, panel_rows, axis=0)
    products = jnp.einsum("isab,iswbc->iswac", a_values, picked, preferred_element_type=jnp.float32)
    pairing = (picked_names[:, :, :, None] == wanted[:, None, None, :]).astype(jnp.float32)

    def partial_terms(offset, amount):
        return jnp.einsum("iswo,iswac->oiac", pairing, products, precision=lax.Precision.HIGHEST)

    return partial_terms


def body(f1_vals, f1_cols, p0_vals, p0_cols, s_vals, s_cols, p1_filter, q_filter):
    layers = lax.axis_size("layer")
    tile_rows = p0_vals.shape[0]
    wanted_first, wanted_second = (
        lax.all_gather(p1_filter, "layer", axis=1, tiled=True),
        lax.all_gather(q_filter, "layer", axis=1, tiled=True),
    )
    a_values, a_columns = (
        lax.all_gather(f1_vals, "col", axis=1, tiled=True),
        lax.all_gather(f1_cols, "col", axis=1, tiled=True),
    )
    p0_panel, p0_names = (
        lax.all_gather(p0_vals, "row", axis=0, tiled=True),
        lax.all_gather(p0_cols, "row", axis=0, tiled=True),
    )
    first_terms = block_terms(
        a_values, a_columns, p0_panel, p0_names, wanted_first, tile_rows, layers
    )
    first_total = lax.psum_scatter(
        first_terms(jnp.int32(0), p1_filter.shape[1] * lax.axis_size("layer")),
        "layer",
        scatter_dimension=0,
        tiled=True,
    )
    p1_local = jnp.transpose(first_total, (1, 0, 2, 3)).astype(jnp.bfloat16)
    b_values, b_columns = (
        lax.all_gather(p1_local, "col", axis=1, tiled=True),
        lax.all_gather(p1_filter, "col", axis=1, tiled=True),
    )
    s_panel, s_names = (
        lax.all_gather(s_vals, "row", axis=0, tiled=True),
        lax.all_gather(s_cols, "row", axis=0, tiled=True),
    )
    second_terms = block_terms(
        b_values, b_columns, s_panel, s_names, wanted_second, tile_rows, layers
    )
    second_total = lax.psum_scatter(
        second_terms(jnp.int32(0), lax.axis_size("layer") * q_filter.shape[1]).astype(jnp.bfloat16),
        "layer",
        scatter_dimension=0,
        tiled=True,
    ).astype(jnp.float32)
    q_local = jnp.transpose(second_total, (1, 0, 2, 3)).astype(jnp.bfloat16)
    return (p1_local, q_local)


def solution(mesh):
    return jax.shard_map(
        body,
        mesh=mesh,
        in_specs=(
            P("row", ("col", "layer"), None, None),
            P("row", ("col", "layer")),
            P(("row", "layer"), "col", None, None),
            P(("row", "layer"), "col"),
            P(("row", "layer"), "col", None, None),
            P(("row", "layer"), "col"),
            P("row", ("col", "layer")),
            P("row", ("col", "layer")),
        ),
        out_specs=(P("row", ("col", "layer"), None, None), P("row", ("col", "layer"), None, None)),
        check_vma=False,
    )
```

profile of v0, /device:TPU:1, one launch (start us, length us, event | category | flops | bytes accessed | tf_op | source)
XLA Modules:
  0.0 369.1 jit_solution(7753233259331326570)
XLA Ops:
  7.2 0.0 all-gather.11.cloned.1.call-start
  7.2 0.7 all-gather.11.cloned.1.call-update
  7.9 0.0 all-gather.13.cloned.1.call-start
  7.9 0.7 all-gather.13.cloned.1.call-update
  8.6 0.0 reduce-scatter.3.cloned.1.call-start
  8.7 4.9 %all-gather.2 = s32[2,2,8]{2,1,0:T(2,128)S(1)} all-gather(s32[1,2,8]{2,1,0:T(2,128)} %bitcast.103), channel_id=1, replica_groups=mesh['row'=16,'col'=8,'layer'=2] {'layer'}, dimensions={0}, use_global_device_ids=true | all-gather | bytes 192 | tf_op jit(solution)/shard_map/all_gather | solution.py:24
  13.6 13.7 %all-gather = s32[8,1,8]{2,1,0:T(1,128)S(1)} all-gather(s32[1,1,8]{2,1,0:T(1,128)} %bitcast.108), channel_id=1, replica_groups=mesh['row'=16,'col'=8,'layer'=2] {'col'}, dimensions={0}, use_global_device_ids=true | all-gather | bytes 288 | tf_op jit(solution)/shard_map/all_gather | solution.py:29
  27.3 0.1 copy.63
  27.4 0.1 reshape.37
  27.5 0.1 copy.62
  27.6 19.2 %all-gather.1 = s32[16,8,2]{1,2,0:T(2,128)S(1)} all-gather(s32[1,8,2]{1,2,0:T(2,128)} %bitcast.105), channel_id=1, replica_groups=mesh['row'=16,'col'=8,'layer'=2] {'row'}, dimensions={0}, use_global_device_ids=true | all-gather | bytes 1088 | tf_op jit(solution)/shard_map/all_gather | solution.py:33
  46.8 0.2 copy.66
  47.0 0.6 gather_fusion.1
  47.6 0.1 copy.88
  47.7 0.1 copy.69
  47.8 42.2 %all-gather.11.cloned.1.call-done = bf16[128,2,128,128]{3,2,1,0:T(8,128)(2,1)} async-done(((bf16[8,2,128,128]{3,2,1,0:T(8,128)(2,1)}), bf16[128,2,128,128]{3,2,1,0:T(8,128)(2,1)}) %all-gather.11.cloned.1.call-update) | async-done | bytes 8388624 | tf_op jit(solution)/shard_map/all_gather | solution.py:32
  90.0 6.4 %gather_fusion = bf16[64,2,128,128]{3,2,1,0:T(8,128)(2,1)} fusion(bf16[128,2,128,128]{3,2,1,0:T(8,128)(2,1)} %all-gather.11.cloned.1.call-done, s32[1024]{0:T(1024)S(1)} %pad_clamp_fusion.1), kind=kCustom, calls=%fused_computation | custom fusion | bytes 8388864 | tf_op jit(solution)/shard_map/jit(_take)/gather | solution.py:9
  96.4 6.4 %copy.64 = bf16[8,8,2,128,128]{3,4,2,1,0:T(8,128)(2,1)} copy(bf16[8,8,2,128,128]{4,3,2,1,0:T(8,128)(2,1)} %bitcast.95) | data formatting | bytes 8388608 | tf_op jit(solution)/shard_map/jit(_take)/gather | solution.py:9
  102.9 26.1 %all-gather.13.cloned.1.call-done = bf16[8,8,128,128]{3,2,1,0:T(8,128)(2,1)} async-done(((bf16[8,1,128,128]{3,2,1,0:T(8,128)(2,1)}), bf16[8,8,128,128]{3,2,1,0:T(8,128)(2,1)}) %all-gather.13.cloned.1.call-update) | async-done | bytes 2097168 | tf_op jit(solution)/shard_map/all_gather | solution.py:28
  129.0 7.4 %fusion.7 = f32[8,8,2,128,128]{3,4,2,1,0:T(8,128)} fusion(bf16[8,8,2,128,128]{3,4,2,1,0:T(8,128)(2,1)} %copy.64, pred[8,8]{1,0:T(8,128)(4,1)S(1)} %copy.62, bf16[8,8,128,128]{3,2,1,0:T(8,128)(2,1)} %all-gather.13.cloned.1.call-done), kind=kOutput, calls=%fused_computation.12 | convolution fusion | flops 538968064 | bytes 14680128 | tf_op jit(solution)/shard_map/isab,iswbc->iswac/dot_general | solution.py:11
  136.4 9.2 %copy.70 = f32[8,8,2,128,128]{4,1,2,3,0:T(8,128)} copy(f32[8,8,2,128,128]{3,4,2,1,0:T(8,128)} %fusion.7) | data formatting | bytes 16777216 | tf_op jit(solution)/shard_map/isab,iswbc->iswac/transpose | solution.py:11
  145.6 0.0 copy-start.3
  145.6 0.0 copy-start.1
  145.6 0.0 copy-start.2
  145.6 6.6 %convolution_bitcast_fusion.1 = f32[4,8,128,128]{3,0,2,1:T(4,128)S(1)} fusion(f32[8,8,2,128,128]{4,1,2,3,0:T(8,128)} %copy.70, s32[8,4]{1,0:T(8,128)S(1)} %copy.69, s32[8,8,2]{1,2,0:T(2,128)S(1)} %copy.68), kind=kOutput, calls=%fused_computation.15 | convolution fusion | flops 100663808 | bytes 10486400 | tf_op jit(solution)/shard_map/iswo,iswac->oiac/dot_general | solution.py:15
  152.2 1.7 copy.71
  153.9 0.0 reduce-scatter.3.cloned.1.call-update
  153.9 0.0 all-gather.15.cloned.1.call-start
  154.0 0.5 all-gather.15.cloned.1.call-update
  154.5 0.0 all-gather.17.cloned.1.call-start
  154.6 17.3 %reduce-scatter.3.cloned.1.call-done = f32[2,8,128,128]{3,2,1,0:T(8,128)} async-done(((f32[4,8,128,128]{3,2,1,0:T(8,128)}), f32[2,8,128,128]{3,2,1,0:T(8,128)}) %reduce-scatter.3.cloned.1.call-update) | async-done | bytes 1048592 | tf_op jit(solution)/shard_map/reduce_scatter | solution.py:38
  171.9 2.1 convert_bitcast_fusion
  174.0 0.0 all-gather.17.cloned.1.call-update
  174.0 0.0 reduce-scatter.5.cloned.1.call-start
  174.1 0.0 copy-done.3
  174.1 1.8 all-gather.5
  175.8 0.0 copy-done.1
  175.8 12.9 %all-gather.3 = s32[8,2,8]{2,1,0:T(2,128)S(1)} all-gather(s32[1,2,8]{2,1,0:T(2,128)S(1)} %bitcast.104), channel_id=1, replica_groups=mesh['row'=16,'col'=8,'layer'=2] {'col'}, dimensions={0}, use_global_device_ids=true | all-gather | bytes 576 | tf_op jit(solution)/shard_map/all_gather | solution.py:47
  188.7 0.1 copy.72
  188.8 0.1 reshape.53
  188.9 0.0 copy-done.2
  188.9 19.2 %all-gather.4 = s32[16,8,2]{1,2,0:T(2,128)S(1)} all-gather(s32[1,8,2]{1,2,0:T(2,128)S(1)} %bitcast.106), channel_id=1, replica_groups=mesh['row'=16,'col'=8,'layer'=2] {'row'}, dimensions={0}, use_global_device_ids=true | all-gather | bytes 1088 | tf_op jit(solution)/shard_map/all_gather | solution.py:51
  208.1 0.2 copy.75
  208.2 0.6 gather_fusion.3
  208.9 0.1 broadcast_select_fusion
  209.0 0.1 copy.76
  209.1 0.1 copy.77
  209.2 41.8 %all-gather.15.cloned.1.call-done = bf16[128,2,128,128]{3,2,1,0:T(8,128)(2,1)} async-done(((bf16[8,2,128,128]{3,2,1,0:T(8,128)(2,1)}), bf16[128,2,128,128]{3,2,1,0:T(8,128)(2,1)}) %all-gather.15.cloned.1.call-update) | async-done | bytes 8388624 | tf_op jit(solution)/shard_map/all_gather | solution.py:50
  251.0 10.0 %gather_fusion.2 = bf16[128,2,128,128]{3,2,1,0:T(8,128)(2,1)} fusion(bf16[128,2,128,128]{3,2,1,0:T(8,128)(2,1)} %all-gather.15.cloned.1.call-done, s32[1024]{0:T(1024)S(1)} %pad_clamp_fusion), kind=kCustom, calls=%fused_computation.2 | custom fusion | bytes 16777728 | tf_op jit(solution)/shard_map/jit(_take)/gather | solution.py:9
  260.9 11.5 %copy.73 = bf16[8,16,2,128,128]{3,4,2,1,0:T(8,128)(2,1)} copy(bf16[8,16,2,128,128]{4,3,2,1,0:T(8,128)(2,1)} %bitcast.94) | data formatting | bytes 16777216 | tf_op jit(solution)/shard_map/jit(_take)/gather | solution.py:9
  272.4 35.5 %all-gather.17.cloned.1.call-done = bf16[8,16,128,128]{3,2,0,1:T(8,128)(2,1)} async-done(((bf16[8,2,128,128]{3,2,0,1:T(8,128)(2,1)}), bf16[8,16,128,128]{3,2,0,1:T(8,128)(2,1)}) %all-gather.17.cloned.1.call-update) | async-done | bytes 4194320 | tf_op jit(solution)/shard_map/all_gather | solution.py:46
  307.9 12.7 %convolution_bitcast_fusion = f32[8,16,2,128,128]{3,4,2,1,0:T(8,128)} fusion(bf16[8,16,2,128,128]{3,4,2,1,0:T(8,128)(2,1)} %copy.73, pred[8,16]{1,0:T(8,128)(4,1)S(1)} %get-tuple-element.10, bf16[8,16,128,128]{3,2,0,1:T(8,128)(2,1)} %all-gather.17.cloned.1.call-done), kind=kOutput, calls=%fused_computation.4 | convolution fusion | flops 1077936128 | bytes 29360256 | tf_op jit(solution)/shard_map/isab,iswbc->iswac/dot_general | solution.py:11
  320.6 17.5 %copy.78 = f32[8,16,2,128,128]{4,1,2,3,0:T(8,128)} copy(f32[8,16,2,128,128]{3,4,2,1,0:T(8,128)} %convolution_bitcast_fusion) | data formatting | bytes 33554432 | tf_op jit(solution)/shard_map/isab,iswbc->iswac/transpose | solution.py:11
  338.1 0.0 copy-start
  338.1 10.4 %fusion.13 = bf16[2,8,128,128]{3,0,2,1:T(2,128)(2,1)S(1)} fusion(f32[8,16,2,128,128]{4,1,2,3,0:T(8,128)} %copy.78, s32[8,2]{1,0:T(8,128)S(1)} %copy.77, s32[8,16,2]{1,2,0:T(2,128)S(1)} %copy.76), kind=kOutput, calls=%fused_computation.18 | convolution fusion | flops 100925952 | bytes 17302592 | tf_op jit(solution)/shard_map/iswo,iswac->oiac/dot_general | solution.py:15
  348.5 0.9 copy.79
  349.4 0.0 reduce-scatter.5.cloned.1.call-update
  349.5 0.0 copy-done
  349.5 0.8 copy.80
  350.3 11.9 %reduce-scatter.5.cloned.1.call-done = bf16[1,8,128,128]{3,2,1,0:T(8,128)(2,1)} async-done(((bf16[2,8,128,128]{3,2,1,0:T(8,128)(2,1)}), bf16[1,8,128,128]{3,2,1,0:T(8,128)(2,1)}) %reduce-scatter.5.cloned.1.call-update) | async-done | bytes 262160 | tf_op jit(solution)/shard_map/reduce_scatter | solution.py:56
  (6 shorter events, 0.1 us)
Async XLA Ops:
  7.2 82.9 %all-gather.11.cloned.1.call-start = ((), (), s32[]{:S(2)}) async-start(), calls=%async_computation.2 | async-start | bytes 8912896 | tf_op jit(solution)/shard_map/all_gather | solution.py:32
  7.9 121.1 %all-gather.13.cloned.1.call-start = ((), (), s32[]{:S(2)}) async-start(), calls=%async_computation.3 | async-start | bytes 2359296 | tf_op jit(solution)/shard_map/all_gather | solution.py:28
  8.6 163.2 %reduce-scatter.3.cloned.1.call-start = ((), (), s32[]{:S(2)}) async-start(), calls=%async_computation.4 | async-start | bytes 3145728 | tf_op jit(solution)/shard_map/reduce_scatter | solution.py:38
  145.6 28.4 %copy-start.3 = (s32[8,1]{0,1:T(1,128)S(1)}, s32[8,1]{0,1:T(1,128)}, u32[]{:S(2)}) copy-start(s32[8,1]{0,1:T(1,128)} %param.15) | copy-start | bytes 100
  145.6 30.2 %copy-start.1 = (s32[8,2]{0,1:T(2,128)S(1)}, s32[8,2]{0,1:T(2,128)}, u32[]{:S(2)}) copy-start(s32[8,2]{0,1:T(2,128)} %param.14) | copy-start | bytes 196
  145.6 43.3 %copy-start.2 = (s32[8,2]{0,1:T(2,128)S(1)}, s32[8,2]{0,1:T(2,128)}, u32[]{:S(2)}) copy-start(s32[8,2]{0,1:T(2,128)} %param.13) | copy-start | bytes 196
  153.9 97.0 %all-gather.15.cloned.1.call-start = ((), (), s32[]{:S(2)}) async-start(), calls=%async_computation.5 | async-start | bytes 8912896 | tf_op jit(solution)/shard_map/all_gather | solution.py:50
  154.5 153.4 %all-gather.17.cloned.1.call-start = ((), (), s32[]{:S(2)}) async-start(), calls=%async_computation.6 | async-start | bytes 4718592 | tf_op jit(solution)/shard_map/all_gather | solution.py:46
  174.0 188.2 %reduce-scatter.5.cloned.1.call-start = ((), (), s32[]{:S(2)}) async-start(), calls=%async_computation.7 | async-start | bytes 786432 | tf_op jit(solution)/shard_map/reduce_scatter | solution.py:56
  338.1 11.4 %copy-start = (bf16[8,2,128,128]{3,2,0,1:T(8,128)(2,1)S(1)}, bf16[8,2,128,128]{3,2,0,1:T(8,128)(2,1)}, u32[]{:S(2)}) copy-start(bf16[8,2,128,128]{3,2,0,1:T(8,128)(2,1)} %convert_bitcast_fusion) | copy-start | bytes 1572868
Sparse Core Ops, SparseCore 0:
  10.4 79.5 all-gather.10
  91.8 37.1 all-gather.12
  154.0 17.7 reduce-scatter.2
  174.5 76.4 all-gather.14
  253.3 54.5 all-gather.16
  349.6 12.6 reduce-scatter.4
where the time goes:
time: 370 us; the launch traced here: 369 us
  waiting for transfers between devices  177 us (48%)
  blocking collectives  71.7 us (19%)
  local copies, waits for them, and re-layouts  66.7 us (18%)
  matrix products  37.2 us (10%)
  between operations  14.2 us (4%)
    all_gather x1, waiting for transfers between devices, body(): lax.all_gather(p0_vals, 'row', axis=0, tiled=True)  42.2 us
    all_gather x1, waiting for transfers between devices, body(): lax.all_gather(s_vals, 'row', axis=0, tiled=True)  41.8 us
    all_gather x1, waiting for transfers between devices, body(): lax.all_gather(p1_local, 'col', axis=1, tiled=True)  35.5 us
    gather x4, local copies, waits for them, and re-layouts, block_terms(): picked = jnp.take(panel, panel_rows, axis=0)  34.3 us
    transpose x2, local copies, waits for them, and re-layouts, block_terms(): jnp.einsum('isab,iswbc->iswac', a_values, picked, preferred_element_type=...  26.7 us
    all_gather x1, waiting for transfers between devices, body(): lax.all_gather(f1_vals, 'col', axis=1, tiled=True)  26.1 us
    dot_general x2, matrix products, block_terms(): jnp.einsum('isab,iswbc->iswac', a_values, picked, preferred_element_type=...  20.1 us
    all_gather x1, blocking collectives, body(): lax.all_gather(p0_cols, 'row', axis=0, tiled=True)  19.2 us
  transfers between devices with their start and end apart: 6, of which 6 were waited for; matrix products, arithmetic and copies ran while one was open for 11% of the time, Pallas kernels for 0%

commit v1 on v0

v1 whole, which is shorter than its diff:
```python
import jax
import jax.numpy as jnp
from jax import lax
from jax.experimental import pallas as pl
from jax.experimental.pallas import tpu as pltpu
from jax.sharding import PartitionSpec as P

MESH = pl.DeviceIdType.MESH
B = 128
SIDE = 4
NZ = 8
ROWS = 8
TILES = SIDE * SIDE
ZERO = TILES * 16
F1C, P0C, SC, P1F, QF = 0, 1, 3, 5, 7


def body_kernel(
    meta_ref, f1_ref, p0_ref, s_ref, p1_ref, q_ref,
    pan, span, f1_all, p1_all, rhs, rhs_q, part, part_in, q_part, q_in,
    meta_row, meta_z, meta_core, row_s, z_s, core_s,
    local_sem, meta_send, meta_recv, pan_send, pan_recv, f1_send, f1_recv,
    part_send, part_recv, p1_send, p1_recv, q_send, q_recv, smem_sem,
):
    r = lax.axis_index("row")
    u = lax.axis_index("col")
    layer = lax.axis_index("layer")
    x, y = r % SIDE, r // SIDE
    other = 1 - layer

    def chip(y_at, x_at):
        return (y_at % SIDE) * SIDE + x_at % SIDE

    own = [
        pltpu.make_async_copy(p0_ref, pan.at[pl.ds(r * 16, 16)], local_sem.at[0]),
        pltpu.make_async_copy(f1_ref, f1_all.at[pl.ds(u * 8, 8)], local_sem.at[1]),
        pltpu.make_async_copy(s_ref, span.at[pl.ds(r * 16, 16)], local_sem.at[2]),
    ]
    for copy in own:
        copy.start()

    barrier = pltpu.get_barrier_semaphore()
    for step in range(1, TILES):
        pl.semaphore_signal(barrier, inc=1, device_id=((r + step) % TILES, u, layer), device_id_type=MESH)
    for step in range(1, NZ):
        pl.semaphore_signal(barrier, inc=1, device_id=(r, (u + step) % NZ, layer), device_id_type=MESH)
    pl.semaphore_signal(barrier, inc=1, device_id=(r, u, other), device_id_type=MESH)

    pan[ZERO] = jnp.zeros((B, B), jnp.bfloat16)
    span[ZERO] = jnp.zeros((B, B), jnp.bfloat16)
    meta_row[r] = meta_ref[...]
    meta_z[u] = meta_ref[...]
    meta_core[layer] = meta_ref[...]
    pl.semaphore_wait(barrier, TILES - 1 + NZ - 1 + 1)

    sent = []

    def send(src, dst, send_sem, recv_sem, device):
        copy = pltpu.make_async_remote_copy(
            src_ref=src, dst_ref=dst, send_sem=send_sem, recv_sem=recv_sem,
            device_id=device, device_id_type=MESH,
        )
        copy.start()
        sent.append(copy)

    def arrived(dst, send_sem, recv_sem, device):
        pltpu.make_async_remote_copy(
            src_ref=dst, dst_ref=dst, send_sem=send_sem, recv_sem=recv_sem,
            device_id=device, device_id_type=MESH,
        ).wait_recv()

    for step in range(1, TILES):
        send(meta_ref, meta_row.at[r], meta_send.at[step], meta_recv.at[step], ((r + step) % TILES, u, layer))
    for step in range(1, NZ):
        at = TILES + step
        send(meta_ref, meta_z.at[u], meta_send.at[at], meta_recv.at[at], (r, (u + step) % NZ, layer))
    send(meta_ref, meta_core.at[layer], meta_send.at[0], meta_recv.at[0], (r, u, other))

    ways = ((0, 1), (0, -1), (1, 1), (1, -1))

    def tile_of(q, along, across):
        first, d = ways[q]
        if first == 0:
            return chip(y - d * across, x - d * along)
        return chip(y - d * along, x - d * across)

    def target(q, phase):
        first, d = ways[q]
        if (first + phase) % 2 == 0:
            return (chip(y, x + d), u, layer)
        return (chip(y + d, x), u, layer)

    def piece(panel, q, along, across):
        return panel.at[pl.ds(tile_of(q, along, across) * 16 + q * 4, 4)]

    def panel_send(which, q, phase, step, j):
        panel = (pan, span)[which]
        at = step if phase == 0 else 3 + step * 4 + j
        part_of = piece(panel, q, step, 0) if phase == 0 else piece(panel, q, j, step)
        send(part_of, part_of, pan_send.at[which, q, at], pan_recv.at[which, q, at], target(q, phase))

    def panel_arrived(which, q, phase, step, j):
        panel = (pan, span)[which]
        at = step if phase == 0 else 3 + step * 4 + j
        part_of = piece(panel, q, step + 1, 0) if phase == 0 else piece(panel, q, j, step + 1)
        arrived(part_of, pan_send.at[which, q, at], pan_recv.at[which, q, at], target(q, phase))

    def panel_begin(which):
        for q in range(4):
            panel_send(which, q, 0, 0, 0)
        for q in range(4):
            panel_send(which, q, 1, 0, 0)

    def panel_round(which, n):
        for q in range(4):
            if n < 3:
                panel_arrived(which, q, 0, n, 0)
                if n < 2:
                    panel_send(which, q, 0, n + 1, 0)
                panel_send(which, q, 1, 0, n + 1)
            else:
                step, j = (n - 3) // 4, (n - 3) % 4
                panel_arrived(which, q, 1, step, j)
                if step < 2:
                    panel_send(which, q, 1, step + 1, j)

    def z_piece(array, width, pieces, e, step):
        d = 1 - 2 * (e % 2)
        size = width // pieces
        return array.at[pl.ds(((u - d * step) % NZ) * width + e * size, size)]

    def z_send(array, width, pieces, sems, e, step):
        d = 1 - 2 * (e % 2)
        part_of = z_piece(array, width, pieces, e, step)
        send(part_of, part_of, sems[0].at[e, step], sems[1].at[e, step], (r, (u + d) % NZ, layer))

    def z_round(array, width, pieces, sems, n):
        for e in range(pieces):
            d = 1 - 2 * (e % 2)
            part_of = z_piece(array, width, pieces, e, n + 1)
            arrived(part_of, sems[0].at[e, n], sems[1].at[e, n], (r, (u + d) % NZ, layer))
            if n + 1 < NZ - 1:
                z_send(array, width, pieces, sems, e, n + 1)

    own[0].wait()
    for q in range(4):
        panel_send(0, q, 0, 0, 0)
    own[1].wait()
    f1_sems, p1_sems = (f1_send, f1_recv), (p1_send, p1_recv)
    for e in range(2):
        z_send(f1_all, 8, 2, f1_sems, e, 0)
    for q in range(4):
        panel_send(0, q, 1, 0, 0)
    own[2].wait()

    for step in range(1, TILES):
        arrived(meta_row.at[(r - step) % TILES], meta_send.at[step], meta_recv.at[step], ((r + step) % TILES, u, layer))
    for step in range(1, NZ):
        at = TILES + step
        arrived(meta_z.at[(u - step) % NZ], meta_send.at[at], meta_recv.at[at], (r, (u + step) % NZ, layer))
    arrived(meta_core.at[other], meta_send.at[0], meta_recv.at[0], (r, u, other))
    tables = [
        pltpu.make_async_copy(meta_row, row_s, smem_sem.at[0]),
        pltpu.make_async_copy(meta_z, z_s, smem_sem.at[1]),
        pltpu.make_async_copy(meta_core, core_s, smem_sem.at[2]),
    ]
    for copy in tables:
        copy.start()

    for n in range(15):
        if n == 11:
            panel_begin(1)
        panel_round(0, n)
        if n < NZ - 1:
            z_round(f1_all, 8, 2, f1_sems, n)
    for copy in tables:
        copy.wait()

    def choose(panel, index):
        return panel[index]

    def first_row(i, carry):
        for c in range(NZ):
            k = z_s[c, i, F1C]
            t = lax.shift_right_logical(k, 4)
            base = t * 16 + c * 2
            n0, n1 = row_s[t, c, P0C], row_s[t, c, P0C + 1]
            for o in range(4):
                want = core_s[o // 2, i, P1F + o % 2]
                index = jnp.where(n0 == want, base, jnp.where(n1 == want, base + 1, ZERO))
                rhs[c * B:(c + 1) * B, o * B:(o + 1) * B] = choose(pan, index)
        lhs = jnp.concatenate([f1_all[c * 8 + i] for c in range(NZ)], axis=1)
        total = jnp.dot(lhs, rhs[...], preferred_element_type=jnp.float32)
        part[0, i] = total[:, :2 * B]
        part[1, i] = total[:, 2 * B:]
        return carry

    def part_send_row(i):
        send(part.at[other, i], part_in.at[i], part_send.at[i], part_recv.at[i], (r, u, other))

    for h in range(4):
        lax.fori_loop(2 * h, 2 * h + 2, first_row, 0)
        part_send_row(2 * h)
        part_send_row(2 * h + 1)
        if h < 3:
            panel_round(1, h)

    def finish_row(i, carry):
        total = (part[layer, i] + part_in[i]).astype(jnp.bfloat16)
        for o in range(2):
            block = total[:, o * B:(o + 1) * B]
            p1_all[u * 16 + i * 2 + o] = block
            p1_ref[i, o] = block
        return carry

    for e in range(4):
        for i in (2 * e, 2 * e + 1):
            arrived(part_in.at[i], part_send.at[i], part_recv.at[i], (r, u, other))
        lax.fori_loop(2 * e, 2 * e + 2, finish_row, 0)
        z_send(p1_all, 16, 4, p1_sems, e, 0)

    for n in range(12):
        panel_round(1, n + 3)
        if n < NZ - 1:
            z_round(p1_all, 16, 4, p1_sems, n)

    def second_row(i, carry):
        for c in range(NZ):
            for a in range(2):
                k = z_s[c, i, P1F + a]
                t = lax.shift_right_logical(k, 4)
                base = t * 16 + c * 2
                n0, n1 = row_s[t, c, SC], row_s[t, c, SC + 1]
                at = c * 2 + a
                for o in range(2):
                    want = core_s[o, i, QF]
                    index = jnp.where(n0 == want, base, jnp.where(n1 == want, base + 1, ZERO))
                    rhs_q[at * B:(at + 1) * B, o * B:(o + 1) * B] = choose(span, index)
        lhs = jnp.concatenate([p1_all[c * 16 + i * 2 + a] for c in range(NZ) for a in range(2)], axis=1)
        total = jnp.dot(lhs, rhs_q[...], preferred_element_type=jnp.float32)
        q_part[0, i] = total[:, :B].astype(jnp.bfloat16)
        q_part[1, i] = total[:, B:].astype(jnp.bfloat16)
        return carry

    for h in range(2):
        lax.fori_loop(4 * h, 4 * h + 4, second_row, 0)
        rows = pl.ds(4 * h, 4)
        send(q_part.at[other, rows], q_in.at[rows], q_send.at[h], q_recv.at[h], (r, u, other))
    for h in range(2):
        rows = pl.ds(4 * h, 4)
        arrived(q_in.at[rows], q_send.at[h], q_recv.at[h], (r, u, other))
        both = q_part[layer, rows].astype(jnp.float32) + q_in[rows].astype(jnp.float32)
        q_ref[rows] = both.astype(jnp.bfloat16)
    for copy in sent:
        copy.wait_send()


def body(f1_vals, f1_cols, p0_vals, p0_cols, s_vals, s_cols, p1_filter, q_filter):
    meta = jnp.concatenate([f1_cols, p0_cols, s_cols, p1_filter, q_filter], axis=1)
    meta = jnp.pad(meta, ((0, 0), (0, B - meta.shape[1])))
    bf16, f32, i32 = jnp.bfloat16, jnp.float32, jnp.int32
    dma = pltpu.SemaphoreType.DMA
    p1, q = pl.pallas_call(
        body_kernel,
        out_shape=(
            jax.ShapeDtypeStruct((ROWS, 2, B, B), bf16),
            jax.ShapeDtypeStruct((ROWS, B, B), bf16),
        ),
        in_specs=[pl.BlockSpec(memory_space=pltpu.VMEM)] + [pl.BlockSpec(memory_space=pl.ANY)] * 3,
        out_specs=(pl.BlockSpec(memory_space=pltpu.VMEM),) * 2,
        scratch_shapes=[
            pltpu.VMEM((TILES * 16 + 1, B, B), bf16),
            pltpu.VMEM((TILES * 16 + 1, B, B), bf16),
            pltpu.VMEM((NZ * 8, B, B), bf16),
            pltpu.VMEM((NZ * 16, B, B), bf16),
            pltpu.VMEM((NZ * B, 4 * B), bf16),
            pltpu.VMEM((NZ * 2 * B, 2 * B), bf16),
            pltpu.VMEM((2, ROWS, B, 2 * B), f32),
            pltpu.VMEM((ROWS, B, 2 * B), f32),
            pltpu.VMEM((2, ROWS, B, B), bf16),
            pltpu.VMEM((ROWS, B, B), bf16),
            pltpu.VMEM((TILES, 8, B), i32),
            pltpu.VMEM((NZ, 8, B), i32),
            pltpu.VMEM((2, 8, B), i32),
            pltpu.SMEM((TILES, 8, B), i32),
            pltpu.SMEM((NZ, 8, B), i32),
            pltpu.SMEM((2, 8, B), i32),
            dma((3,)),
            dma((TILES + NZ,)), dma((TILES + NZ,)),
            dma((2, 4, 15)), dma((2, 4, 15)),
            dma((2, NZ - 1)), dma((2, NZ - 1)),
            dma((ROWS,)), dma((ROWS,)),
            dma((4, NZ - 1)), dma((4, NZ - 1)),
            dma((2,)), dma((2,)),
            dma((3,)),
        ],
        compiler_params=pltpu.CompilerParams(
            collective_id=0, has_side_effects=True, vmem_limit_bytes=56 * 1024 * 1024
        ),
    )(
        meta,
        f1_vals.reshape(ROWS, B, B),
        p0_vals.reshape(16, B, B),
        s_vals.reshape(16, B, B),
    )
    return p1, q.reshape(ROWS, 1, B, B)


def solution(mesh):
    return jax.shard_map(
        body,
        mesh=mesh,
        in_specs=(
            P("row", ("col", "layer"), None, None),
            P("row", ("col", "layer")),
            P(("row", "layer"), "col", None, None),
            P(("row", "layer"), "col"),
            P(("row", "layer"), "col", None, None),
            P(("row", "layer"), "col"),
            P("row", ("col", "layer")),
            P("row", ("col", "layer")),
        ),
        out_specs=(P("row", ("col", "layer"), None, None), P("row", ("col", "layer"), None, None)),
        check_vma=False,
    )
```

time: 370 us -> 146 us (0.39)
  waiting for transfers between devices: 177 us -> 0 us
  Pallas kernels: 0 us -> 138 us
  blocking collectives: 71.7 us -> 0 us
  local copies, waits for them, and re-layouts: 66.7 us -> 6.73 us
  matrix products: 37.2 us -> 0 us
  between operations: 14.2 us -> 0.66 us
    all_gather x4 -> x0, waiting for transfers between devices: 146 us -> none  [the longest x1 42.2 us: body(): lax.all_gather(p0_vals, 'row', axis=0, tiled=True)]
    pallas_call x0 -> x1, Pallas kernels: none -> 138 us  [body(): pl.pallas_call(body_kernel, out_shape=(jax.ShapeDtypeStruct((ROWS, 2, B,...]
    all_gather x6 -> x0, blocking collectives: 71.7 us -> none  [the longest x1 19.2 us: body(): lax.all_gather(p0_cols, 'row', axis=0, tiled=True)]
    dot_general x4 -> x0, matrix products: 37.2 us -> none  [the longest x2 20.1 us: block_terms(): jnp.einsum('isab,iswbc->iswac', a_values, picked, preferred_element_type=...]
    gather x7 -> x0, local copies, waits for them, and re-layouts: 35.7 us -> none  [the longest x4 34.3 us: block_terms(): picked = jnp.take(panel, panel_rows, axis=0)]
    reduce_scatter x2 -> x0, waiting for transfers between devices: 29.3 us -> none  [the longest x1 17.3 us: body(): lax.psum_scatter(first_terms(jnp.int32(0), p1_filter.shape[1] * lax.axis_...]
    transpose x3 -> x0, local copies, waits for them, and re-layouts: 28.3 us -> none  [the longest x2 26.7 us: block_terms(): jnp.einsum('isab,iswbc->iswac', a_values, picked, preferred_element_type=...]
    unnamed x12 -> x19, local copies, waits for them, and re-layouts: 1.07 us -> 6.05 us
  transfers between devices with their start and end apart: 6 -> 0, of which waited for: 6 -> 0; matrix products, arithmetic and copies ran while one was open for 11% -> 0% of each run, Pallas kernels for 0% -> 0%
where the time goes in v1:
time: 146 us
  Pallas kernels  138 us (95%)
  local copies, waits for them, and re-layouts  6.73 us (5%)
    pallas_call x1, Pallas kernels, body(): pl.pallas_call(body_kernel, out_shape=(jax.ShapeDtypeStruct((ROWS, 2, B,...  138 us
    unnamed x19, local copies, waits for them, and re-layouts  6.05 us

profile of v1, /device:TPU:1, one launch (start us, length us, event | category | flops | bytes accessed | tf_op | source)
XLA Modules:
  0.0 145.6 jit_solution(11950383983439601112)
XLA Ops:
  0.6 0.0 copy-start.4
  0.6 0.6 copy-done.4
  1.3 0.0 copy-start.1
  1.3 0.1 copy.10
  1.4 0.6 copy-done.1
  2.0 0.0 copy-start.2
  2.0 0.1 copy.11
  2.0 0.6 copy-done.2
  2.6 0.0 copy-start.3
  2.6 0.1 copy.12
  2.7 0.6 copy-done.3
  3.3 0.0 copy-start.5
  3.3 0.1 copy.13
  3.4 0.6 copy-done.5
  4.0 0.1 copy.14
  4.1 0.1 concatenate.3
  4.1 0.6 pad.4.meta_ref
  4.7 138.2 %shard_map.95 = (bf16[8,2,128,128]{3,2,1,0:T(8,128)(2,1)}, bf16[8,128,128]{2,1,0:T(8,128)(2,1)}) custom-call(s32[8,128]{1,0:T(8,128)} %pad.4.meta_ref, bf16[8,128,128]{2,1,0:T(8,128)(2,1)} %bitcast.8, bf16[16,128,128]{2,1,0:T(8,128)(2,1)} %bitcast.6, bf16[16,128,128]{2,1,0:T(8,128)(2,1)} %bitcast.7), custom_call_target="tpu_custom_call" | custom-call | tf_op jit(solution)/shard_map/pallas_call | solution.py:263
  142.9 0.0 copy-start
  142.9 1.9 %copy.18 = bf16[8,2,128,128]{3,2,1,0:T(8,128)(2,1)} copy(bf16[8,2,128,128]{3,2,1,0:T(8,128)(2,1)} %get-tuple-element.10) | data formatting | bytes 1048576
  144.8 0.0 copy-done
  144.9 0.7 copy.19
Async XLA Ops:
  0.6 0.7 copy-start.4
  1.3 0.7 copy-start.1
  2.0 0.7 copy-start.2
  2.6 0.7 copy-start.3
  3.3 0.7 copy-start.5
  142.9 1.9 %copy-start = (bf16[8,128,128]{2,1,0:T(8,128)(2,1)S(1)}, bf16[8,128,128]{2,1,0:T(8,128)(2,1)}, u32[]{:S(2)}) copy-start(bf16[8,128,128]{2,1,0:T(8,128)(2,1)} %get-tuple-element.5) | copy-start | bytes 786436

commit v2 on v1

--- a/solution.py
+++ b/solution.py
@@ -11,11 +11,521 @@
 NZ = 8
 ROWS = 8
 TILES = SIDE * SIDE
+CAP = 12
+HALF = CAP // 2
+PACKED = 65
+BLOCKS = PACKED + 6 * CAP
+F32, I32, BF16 = jnp.float32, jnp.int32, jnp.bfloat16
+
+
+def inside(index, count):
+    return lax.max(lax.min(index, count - 1), 0)
+
+
+def fast_kernel(
+    f1c_ref, p0c_ref, sc_ref, p1f_ref, qf_ref, f1_ref, p0_ref, s_ref, p1_ref, q_ref, flag_ref,
+    whole_p, whole_s, buf_p, buf_s, outs, relays, f1_all, p1_all, rhs, rhs_q, part, part_in, q_part, q_in,
+    own_tile, row_tiles, z_tiles, core_tiles, demand, code, code_in, index_v, list_v, index_s, list_s,
+    flag_own, flag_row, flag_z, flag_core,
+    local_sem, meta_send, meta_recv, code_send, code_recv, pan_send, pan_recv, pack_send, pack_recv,
+    rel_send, rel_recv, f1_send, f1_recv, part_send, part_recv, p1_send, p1_recv, q_send, q_recv,
+    flag_send, flag_recv, smem_sem,
+):
+    r = lax.axis_index("row")
+    u = lax.axis_index("col")
+    layer = lax.axis_index("layer")
+    x, y = r % SIDE, r // SIDE
+    other = 1 - layer
+    whole, bufs = (whole_p, whole_s), (buf_p, buf_s)
+
+    def chip(y_at, x_at):
+        return ((y_at % SIDE) * SIDE + x_at % SIDE, u, layer)
+
+    own = []
+    for which, ref in ((0, p0_ref), (1, s_ref)):
+        own.append(pltpu.make_async_copy(ref.at[pl.ds(0, 8)], whole[which].at[pl.ds(1 + x * 8, 8)], local_sem.at[2 * which]))
+        own.append(pltpu.make_async_copy(ref.at[pl.ds(8, 8)], whole[which].at[pl.ds(33 + y * 8, 8)], local_sem.at[2 * which + 1]))
+    own.append(pltpu.make_async_copy(f1_ref, f1_all.at[pl.ds(u * 8, 8)], local_sem.at[4]))
+    for copy in own:
+        copy.start()
+
+    barrier = pltpu.get_barrier_semaphore()
+    for step in range(1, TILES):
+        pl.semaphore_signal(barrier, inc=1, device_id=((r + step) % TILES, u, layer), device_id_type=MESH)
+    for step in range(1, NZ):
+        pl.semaphore_signal(barrier, inc=1, device_id=(r, (u + step) % NZ, layer), device_id_type=MESH)
+    pl.semaphore_signal(barrier, inc=1, device_id=(r, u, other), device_id_type=MESH)
+
+    for panel in whole:
+        panel[0] = jnp.zeros((B, B), BF16)
+    sub8 = lax.broadcasted_iota(I32, (8, B), 0)
+    lane8 = lax.broadcasted_iota(I32, (8, B), 1)
+
+    own_tile[...] = jnp.full((8, B), -1, I32)
+    for at, ref in ((0, p0c_ref), (2, sc_ref), (4, f1c_ref), (5, p1f_ref), (7, qf_ref)):
+        own_tile[at:at + ref.shape[0], 0:8] = ref[...]
+    row_tiles[r] = own_tile[...]
+    z_tiles[u] = own_tile[...]
+    core_tiles[layer] = own_tile[...]
+    pl.semaphore_wait(barrier, TILES - 1 + NZ - 1 + 1)
+
+    sent = []
+
+    def remote(src, dst, send_sem, recv_sem, device):
+        return pltpu.make_async_remote_copy(
+            src_ref=src, dst_ref=dst, send_sem=send_sem, recv_sem=recv_sem,
+            device_id=device, device_id_type=MESH,
+        )
+
+    def send(src, dst, send_sem, recv_sem, device):
+        copy = remote(src, dst, send_sem, recv_sem, device)
+        copy.start()
+        sent.append(copy)
+
+    def arrived(dst, send_sem, recv_sem, device):
+        remote(dst, dst, send_sem, recv_sem, device).wait_recv()
+
+    def row_peer(step):
+        return ((r + step) % TILES, u, layer)
+
+    def z_peer(step):
+        return (r, (u + step) % NZ, layer)
+
+    core_peer = (r, u, other)
+
+    for step in range(1, NZ):
+        at = TILES + step
+        send(own_tile, z_tiles.at[u], meta_send.at[at], meta_recv.at[at], z_peer(step))
+    send(own_tile, core_tiles.at[layer], meta_send.at[0], meta_recv.at[0], core_peer)
+    for step in range(1, TILES):
+        send(own_tile, row_tiles.at[r], meta_send.at[step], meta_recv.at[step], row_peer(step))
+
+    def along(axis, d):
+        return chip(y, x + d) if axis == 0 else chip(y + d, x)
+
+    def quarter(which, h, q, d):
+        at = (x if h == 0 else y) - d
+        return whole[which].at[pl.ds(1 + 32 * h + (at % SIDE) * 8 + q * 4, 4)]
+
+    def panel_begin(which):
+        for n in range(2):
+            for h in range(2):
+                for way in (0, 1):
+                    q, d = n if way == 0 else 1 - n, 1 - 2 * way
+                    part_of = quarter(which, h, q, 0)
+                    send(part_of, part_of, pan_send.at[which, h, way, n], pan_recv.at[which, h, way, n], along(h, d))
+
+    def panel_round(which, n):
+        for h in range(2):
+            for way in (0, 1):
+                d = 1 - 2 * way
+                q = (n if way == 0 else 1 - n) if n < 2 else way
+                part_of = quarter(which, h, q, d if n < 2 else 2 * d)
+                arrived(part_of, pan_send.at[which, h, way, n], pan_recv.at[which, h, way, n], along(h, d))
+                if n == 0:
+                    send(part_of, part_of, pan_send.at[which, h, way, 2], pan_recv.at[which, h, way, 2], along(h, d))
+
+    def packet(which, h, d):
+        return bufs[which].at[pl.ds(PACKED + (h * 3 + d - 1) * CAP, CAP)]
+
+    def half_of(ref, e):
+        return ref.at[pl.ds(e * HALF, HALF)]
+
+    def relay(which):
+        for h in range(2):
+            for e, way in ((0, 1), (1, -1)):
+                arrived(relays.at[which, h, e], rel_send.at[which, h, e], rel_recv.at[which, h, e], along(1 - h, way))
+                send(
+                    relays.at[which, h, e], half_of(packet(which, h, 2), e),
+                    pack_send.at[which, h, 3 + e], pack_recv.at[which, h, 3 + e], along(1 - h, way),
+                )
+
+    def packets_arrived(which):
+        for h in range(2):
+            for d in (1, 3):
+                arrived(packet(which, h, d), pack_send.at[which, h, d - 1], pack_recv.at[which, h, d - 1], along(1 - h, 1))
+            for e in range(2):
+                arrived(half_of(packet(which, h, 2), e), pack_send.at[which, h, 3 + e], pack_recv.at[which, h, 3 + e], along(1 - h, 1))
+
+    def z_piece(array, width, pieces, e, step):
+        d = 1 - 2 * (e % 2)
+        size = width // pieces
+        return array.at[pl.ds(((u - d * step) % NZ) * width + e * size, size)]
+
+    def z_send(array, width, pieces, sems, e, step):
+        d = 1 - 2 * (e % 2)
+        part_of = z_piece(array, width, pieces, e, step)
+        send(part_of, part_of, sems[0].at[e, step], sems[1].at[e, step], z_peer(d))
+
+    def z_round(array, width, pieces, sems, n, only=None):
+        for e in range(pieces) if only is None else only:
+            d = 1 - 2 * (e % 2)
+            arrived(z_piece(array, width, pieces, e, n + 1), sems[0].at[e, n], sems[1].at[e, n], z_peer(d))
+            if n + 1 < NZ - 1:
+                z_send(array, width, pieces, sems, e, n + 1)
+
+    f1_sems, p1_sems = (f1_send, f1_recv), (p1_send, p1_recv)
+    own[0].wait()
+    own[1].wait()
+    panel_begin(0)
+    own[4].wait()
+    for e in range(4):
+        z_send(f1_all, 8, 4, f1_sems, e, 0)
+    own[2].wait()
+    own[3].wait()
+
+    for step in range(1, NZ):
+        at = TILES + step
+        arrived(z_tiles.at[(u - step) % NZ], meta_send.at[at], meta_recv.at[at], z_peer(step))
+    arrived(core_tiles.at[other], meta_send.at[0], meta_recv.at[0], core_peer)
+
+    def column_of(line):
+        spread = jnp.where(sub8 == lane8, jnp.broadcast_to(line.astype(F32), (8, B)), 0.0)
+        return jnp.broadcast_to(jnp.sum(spread, axis=1, keepdims=True), (8, B))
+
+    for at in range(3):
+        merged = jnp.zeros((8, B), F32)
+        for c in range(NZ):
+            merged = jnp.where(lane8 == c, column_of(z_tiles[c, 4 + at:5 + at, :]), merged)
+        demand[at] = merged.astype(I32)
+    for o in range(4):
+        demand[3 + o] = column_of(core_tiles[o // 2, 5 + o % 2:6 + o % 2, :]).astype(I32)
+    for o in range(2):
+        demand[7 + o] = column_of(core_tiles[o, 7:8, :]).astype(I32)
+
+    for step in range(1, TILES):
+        arrived(row_tiles.at[(r - step) % TILES], meta_send.at[step], meta_recv.at[step], row_peer(step))
+
+    tile = lax.broadcasted_iota(I32, (TILES, B), 0)
+    lane = lax.broadcasted_iota(I32, (TILES, B), 1)
+    tile_y, tile_x = lax.shift_right_logical(tile, 2), tile & 3
+    upper = lane >= 4
+    lane_a = lax.broadcasted_iota(I32, (B, B), 0)
+    lane_b = lax.broadcasted_iota(I32, (B, B), 1)
+    same = lax.shift_right_logical(lane_a, 2) == lax.shift_right_logical(lane_b, 2)
+    one, nil = jnp.ones((), F32), jnp.zeros((), F32)
+    lanes_all = jnp.where(same, one, nil)
+    lanes_before = jnp.where(same & (lane_a < lane_b), one, nil)
+    tile_a = lax.broadcasted_iota(I32, (TILES, TILES), 0)
+    tile_b = lax.broadcasted_iota(I32, (TILES, TILES), 1)
+    before = tile_b < tile_a
+    same_y = lax.shift_right_logical(tile_a, 2) == lax.shift_right_logical(tile_b, 2)
+    same_x = (tile_a & 3) == (tile_b & 3)
+    tiles_y = jnp.where(before & same_y, one, nil)
+    tiles_x = jnp.where(before & same_x, one, nil)
+
+    def dot(a, b):
+        return jnp.dot(a, b, preferred_element_type=F32)
+
+    name = [[row_tiles[:, 2 * which + w, :] for w in range(2)] for which in range(2)]
+
+    def wide(at, i):
+        return jnp.broadcast_to(demand[at, i:i + 1, :], (TILES, B))
+
+    def matches(which):
+        result = []
+        for i in range(ROWS):
+            wants = [wide(at, i) for at in (range(3, 7) if which == 0 else range(7, 9))]
+            for at in (range(1) if which == 0 else range(1, 3)):
+                hit = lax.shift_right_logical(wide(at, i), 4) == tile
+                result.append([[hit & (name[which][w] == want) for w in range(2)] for want in wants])
+        return result
+
+    def needs(masks):
+        total = []
+        for w in range(2):
+            need = masks[0][0][w]
+            for row in masks:
+                for slot in row:
+                    need = need | slot[w]
+            total.append(jnp.where(need, one, nil))
+        return total
+
+    def ranks(need):
+        both = need[0] + need[1]
+        all_of = dot(both, lanes_all)
+        first = jnp.where(upper, dot(tiles_x, all_of), dot(tiles_y, all_of)) + dot(both, lanes_before)
+        return [first, first + need[0]]
+
+    within = (lane & 3) * 2
+    place = 1 + jnp.where(upper, 32 + tile_y * 8 + within, tile_x * 8 + within)
+    offset = jnp.where(upper, tile_x - x, tile_y - y) & 3
+    here = offset == 0
+    packed = PACKED + jnp.where(upper, 3 * CAP, 0) + (offset - 1) * CAP
+    place_f, packed_f = place.astype(F32), packed.astype(F32)
+
+    def own_code(which):
+        masks = matches(which)
+        need = needs(masks)
+        rank = ranks(need)
+        code[which] = (jnp.where(need[0] > 0.5, rank[0] + 1.0, 0.0) + 64.0 * jnp.where(need[1] > 0.5, rank[1] + 1.0, 0.0)).astype(I32)
+        for axis in range(2):
+            for d in (1, 2, 3):
+                at = axis * 3 + d - 1
+                send(
+                    code.at[which], code_in.at[which, axis, 3 - d],
+                    code_send.at[which, at], code_recv.at[which, axis * 3 + 3 - d], along(axis, d),
+                )
+        return masks, need, rank
+
+    def own_index(which, masks, need, rank):
+        spot, worst = [], jnp.zeros((TILES, B), F32)
+        for w in range(2):
+            fits = rank[w] < float(CAP)
+            spot.append(jnp.where(here, place_f + float(w), jnp.where(fits, packed_f + rank[w], 0.0)))
+            worst = worst + jnp.where((need[w] > 0.5) & jnp.logical_not(fits | here), one, nil)
+        at = 0
+        for row in masks:
+            for slot in row:
+                chosen = jnp.where(slot[0], spot[0], jnp.where(slot[1], spot[1], 0.0))
+                line = jnp.sum(chosen, axis=0, keepdims=True)
+                index_v[which, at:at + 1, :] = line.astype(I32)
+                at += 1
+        return worst
+
+    def peer_lists(which):
+        table = jnp.zeros((TILES, B), F32)
+        for h in range(2):
+            axis = 1 - h
+            mine = (jnp.logical_not(upper) & (tile_y == y)) if h == 0 else (upper & (lane < 8) & (tile_x == x))
+            for d in (1, 2, 3):
+                at = axis * 3 + d - 1
+                arrived(code_in.at[which, axis, d - 1], code_send.at[which, at], code_recv.at[which, at], along(axis, d))
+                there = jnp.where(mine, code_in[which, axis, d - 1], 0)
+                rank = [there & 63, lax.shift_right_logical(there, 6)]
+                slots = jnp.zeros((TILES, B), F32)
+                for j in range(CAP):
+                    chosen = jnp.where(rank[0] == j + 1, place_f, 0.0) + jnp.where(rank[1] == j + 1, place_f + 1.0, 0.0)
+                    line = jnp.sum(chosen, axis=0, keepdims=True)
+                    slots = jnp.where(tile == j, jnp.broadcast_to(line, (TILES, B)), slots)
+                column = jnp.broadcast_to(jnp.sum(slots, axis=1, keepdims=True), (TILES, B))
+                table = jnp.where(lane == (which * 2 + h) * 3 + d - 1, column, table)
+        return table
+
+    found = own_code(0)
+    found_s = own_code(1)
+    panel_round(0, 0)
+    z_round(f1_all, 8, 4, f1_sems, 0)
+    lists = [pltpu.make_async_copy(list_v.at[w], list_s.at[w], smem_sem.at[w]) for w in range(2)]
+    list_v[0] = peer_lists(0).astype(I32)
+    lists[0].start()
+    z_round(f1_all, 8, 4, f1_sems, 1)
+    panel_round(0, 1)
+    panel_round(0, 2)
+    settle = [pltpu.make_async_copy(whole[w], bufs[w].at[pl.ds(0, PACKED)], local_sem.at[5 + w]) for w in range(2)]
+    z_round(f1_all, 8, 4, f1_sems, 2)
+    lists[0].wait()
+
+    def pack(which, ref):
+        for h in range(2):
+            for d in (2, 1, 3):
+                column = (which * 2 + h) * 3 + d - 1
+                for j in range(CAP):
+                    outs[which, h, d - 1, j] = whole[which][inside(ref[j, column], PACKED)]
+                axis = 1 - h
+                if d == 2:
+                    for e, way in ((0, 1), (1, -1)):
+                        send(
+                            half_of(outs.at[which, h, 1], e), relays.at[which, h, e],
+                            rel_send.at[which, h, e], rel_recv.at[which, h, e], along(axis, way),
+                        )
+                else:
+                    way = 1 if d == 1 else -1
+                    send(
+                        outs.at[which, h, d - 1], packet(which, h, 4 - d),
+                        pack_send.at[which, h, d - 1], pack_recv.at[which, h, 3 - d], along(axis, way),
+                    )
+
+    pack(0, list_s.at[0])
+    settle[0].start()
+    z_round(f1_all, 8, 4, f1_sems, 3)
+    over = own_index(0, *found)
+    first_index = pltpu.make_async_copy(index_v.at[0], index_s.at[0], smem_sem.at[2])
+    first_index.start()
+    list_v[1] = peer_lists(1).astype(I32)
+    lists[1].start()
+    z_round(f1_all, 8, 4, f1_sems, 4)
+    relay(0)
+    panel_begin(1)
+    z_round(f1_all, 8, 4, f1_sems, 5)
+    over = over + own_index(1, *found_s)
+    second_index = pltpu.make_async_copy(index_v.at[1], index_s.at[1], smem_sem.at[3])
+    second_index.start()
+    flag_own[0] = over[:8] + over[8:]
+    z_round(f1_all, 8, 4, f1_sems, 6)
+    first_index.wait()
+    settle[0].wait()
+    packets_arrived(0)
+    lists[1].wait()
+
+    def first_row(i, carry):
+        for c in range(NZ):
+            for o in range(4):
+                rhs[c * B:(c + 1) * B, o * B:(o + 1) * B] = buf_p[inside(index_s[0, i * 4 + o, c], BLOCKS)]
+        lhs = jnp.concatenate([f1_all[c * 8 + i] for c in range(NZ)], axis=1)
+        total = dot(lhs, rhs[...])
+        part[0, i] = total[:, :2 * B]
+        part[1, i] = total[:, 2 * B:]
+        return carry
+
+    def part_send_row(i):
+        send(part.at[other, i], part_in.at[i], part_send.at[i], part_recv.at[i], core_peer)
+
+    def finish_row(i, carry):
+        total = (part[layer, i] + part_in[i]).astype(BF16)
+        for o in range(2):
+            block = total[:, o * B:(o + 1) * B]
+            p1_all[u * 16 + i * 2 + o] = block
+            p1_ref[i, o] = block
+        return carry
+
+    def finish(e):
+        for i in (2 * e, 2 * e + 1):
+            arrived(part_in.at[i], part_send.at[i], part_recv.at[i], core_peer)
+        lax.fori_loop(2 * e, 2 * e + 2, finish_row, 0)
+        z_send(p1_all, 16, 4, p1_sems, e, 0)
+
+    for h in range(4):
+        lax.fori_loop(2 * h, 2 * h + 2, first_row, 0)
+        part_send_row(2 * h)
+        part_send_row(2 * h + 1)
+        if h > 0:
+            finish(h - 1)
+    finish(3)
+
+    for step in range(1, TILES):
+        send(flag_own.at[0], flag_row.at[step - 1], flag_send.at[step - 1], flag_recv.at[step - 1], row_peer(step))
+    z_round(p1_all, 16, 4, p1_sems, 0)
+    for n in range(3):
+        panel_round(1, n)
+    pack(1, list_s.at[1])
+    settle[1].start()
+    z_round(p1_all, 16, 4, p1_sems, 1)
+    total = flag_own[0]
+    for step in range(1, TILES):
+        arrived(flag_row.at[step - 1], flag_send.at[step - 1], flag_recv.at[step - 1], row_peer(step))
+        total = total + flag_row[step - 1]
+    flag_own[1] = total
+    for step in range(1, NZ):
+        at = TILES - 2 + step
+        send(flag_own.at[1], flag_z.at[step - 1], flag_send.at[at], flag_recv.at[at], z_peer(step))
+    z_round(p1_all, 16, 4, p1_sems, 2)
+    relay(1)
+    z_round(p1_all, 16, 4, p1_sems, 3)
+    for step in range(1, NZ):
+        at = TILES - 2 + step
+        arrived(flag_z.at[step - 1], flag_send.at[at], flag_recv.at[at], z_peer(step))
+        total = total + flag_z[step - 1]
+    flag_own[2] = total
+    at = TILES + NZ - 2
+    send(flag_own.at[2], flag_core, flag_send.at[at], flag_recv.at[at], core_peer)
+    z_round(p1_all, 16, 4, p1_sems, 4)
+    arrived(flag_core, flag_send.at[at], flag_recv.at[at], core_peer)
+    total = jnp.sum(total + flag_core[...], axis=0, keepdims=True)
+    total = jnp.sum(total, axis=1, keepdims=True)
+    flag_ref[...] = jnp.broadcast_to(total, (8, B))
+    z_round(p1_all, 16, 4, p1_sems, 5)
+    packets_arrived(1)
+    settle[1].wait()
+    second_index.wait()
+
+    def second_row(i, carry):
+        for c in range(NZ):
+            for a in range(2):
+                at = c * 2 + a
+                for o in range(2):
+                    rhs_q[at * B:(at + 1) * B, o * B:(o + 1) * B] = buf_s[inside(index_s[1, i * 4 + a * 2 + o, c], BLOCKS)]
+        lhs = jnp.concatenate([p1_all[c * 16 + i * 2 + a] for c in range(NZ) for a in range(2)], axis=1)
+        total = dot(lhs, rhs_q[...])
+        q_part[0, i] = total[:, :B].astype(BF16)
+        q_part[1, i] = total[:, B:].astype(BF16)
+        return carry
+
+    for h in range(4):
+        z_round(p1_all, 16, 4, p1_sems, NZ - 2, (h,))
+        lax.fori_loop(2 * h, 2 * h + 2, second_row, 0)
+        rows = pl.ds(2 * h, 2)
+        send(q_part.at[other, rows], q_in.at[rows], q_send.at[h], q_recv.at[h], core_peer)
+    for h in range(4):
+        rows = pl.ds(2 * h, 2)
+        arrived(q_in.at[rows], q_send.at[h], q_recv.at[h], core_peer)
+        both = q_part[layer, rows].astype(F32) + q_in[rows].astype(F32)
+        q_ref[rows] = both.astype(BF16)
+    for copy in sent:
+        copy.wait_send()
+
+
+def fast(f1_vals, f1_cols, p0_vals, p0_cols, s_vals, s_cols, p1_filter, q_filter):
+    dma = pltpu.SemaphoreType.DMA
+    vmem = pl.BlockSpec(memory_space=pltpu.VMEM)
+    return pl.pallas_call(
+        fast_kernel,
+        out_shape=(
+            jax.ShapeDtypeStruct((ROWS, 2, B, B), BF16),
+            jax.ShapeDtypeStruct((ROWS, B, B), BF16),
+            jax.ShapeDtypeStruct((8, B), F32),
+        ),
+        in_specs=[vmem] * 5 + [pl.BlockSpec(memory_space=pl.ANY)] * 3,
+        out_specs=(vmem,) * 3,
+        scratch_shapes=[
+            pltpu.VMEM((PACKED, B, B), BF16),
+            pltpu.VMEM((PACKED, B, B), BF16),
+            pltpu.VMEM((BLOCKS, B, B), BF16),
+            pltpu.VMEM((BLOCKS, B, B), BF16),
+            pltpu.VMEM((2, 2, 3, CAP, B, B), BF16),
+            pltpu.VMEM((2, 2, 2, HALF, B, B), BF16),
+            pltpu.VMEM((NZ * 8, B, B), BF16),
+            pltpu.VMEM((NZ * 16, B, B), BF16),
+            pltpu.VMEM((NZ * B, 4 * B), BF16),
+            pltpu.VMEM((NZ * 2 * B, 2 * B), BF16),
+            pltpu.VMEM((2, ROWS, B, 2 * B), F32),
+            pltpu.VMEM((ROWS, B, 2 * B), F32),
+            pltpu.VMEM((2, ROWS, B, B), BF16),
+            pltpu.VMEM((ROWS, B, B), BF16),
+            pltpu.VMEM((8, B), I32),
+            pltpu.VMEM((TILES, 8, B), I32),
+            pltpu.VMEM((NZ, 8, B), I32),
+            pltpu.VMEM((2, 8, B), I32),
+            pltpu.VMEM((9, 8, B), I32),
+            pltpu.VMEM((2, TILES, B), I32),
+            pltpu.VMEM((2, 2, 3, TILES, B), I32),
+            pltpu.VMEM((2, 32, B), I32),
+            pltpu.VMEM((2, TILES, B), I32),
+            pltpu.SMEM((2, 32, B), I32),
+            pltpu.SMEM((2, TILES, B), I32),
+            pltpu.VMEM((3, 8, B), F32),
+            pltpu.VMEM((TILES - 1, 8, B), F32),
+            pltpu.VMEM((NZ - 1, 8, B), F32),
+            pltpu.VMEM((8, B), F32),
+            dma((7,)),
+            dma((TILES + NZ,)), dma((TILES + NZ,)),
+            dma((2, 6)), dma((2, 6)),
+            dma((2, 2, 2, 3)), dma((2, 2, 2, 3)),
+            dma((2, 2, 5)), dma((2, 2, 5)),
+            dma((2, 2, 2)), dma((2, 2, 2)),
+            dma((4, NZ - 1)), dma((4, NZ - 1)),
+            dma((ROWS,)), dma((ROWS,)),
+            dma((4, NZ - 1)), dma((4, NZ - 1)),
+            dma((4,)), dma((4,)),
+            dma((TILES + NZ - 1,)), dma((TILES + NZ - 1,)),
+            dma((4,)),
+        ],
+        compiler_params=pltpu.CompilerParams(
+            collective_id=0, has_side_effects=True, vmem_limit_bytes=56 * 1024 * 1024
+        ),
+    )(
+        f1_cols.T, p0_cols.T, s_cols.T, p1_filter.T, q_filter.T,
+        f1_vals.reshape(ROWS, B, B),
+        p0_vals.reshape(16, B, B),
+        s_vals.reshape(16, B, B),
+    )
+
+
 ZERO = TILES * 16
 F1C, P0C, SC, P1F, QF = 0, 1, 3, 5, 7
 
 
-def body_kernel(
+def dense_kernel(
     meta_ref, f1_ref, p0_ref, s_ref, p1_ref, q_ref,
     pan, span, f1_all, p1_all, rhs, rhs_q, part, part_in, q_part, q_in,
     meta_row, meta_z, meta_core, row_s, z_s, core_s,
@@ -255,13 +765,13 @@
         copy.wait_send()
 
 
-def body(f1_vals, f1_cols, p0_vals, p0_cols, s_vals, s_cols, p1_filter, q_filter):
+def dense(f1_vals, f1_cols, p0_vals, p0_cols, s_vals, s_cols, p1_filter, q_filter):
     meta = jnp.concatenate([f1_cols, p0_cols, s_cols, p1_filter, q_filter], axis=1)
     meta = jnp.pad(meta, ((0, 0), (0, B - meta.shape[1])))
     bf16, f32, i32 = jnp.bfloat16, jnp.float32, jnp.int32
     dma = pltpu.SemaphoreType.DMA
     p1, q = pl.pallas_call(
-        body_kernel,
+        dense_kernel,
         out_shape=(
             jax.ShapeDtypeStruct((ROWS, 2, B, B), bf16),
             jax.ShapeDtypeStruct((ROWS, B, B), bf16),
@@ -295,7 +805,7 @@
             dma((3,)),
         ],
         compiler_params=pltpu.CompilerParams(
-            collective_id=0, has_side_effects=True, vmem_limit_bytes=56 * 1024 * 1024
+            collective_id=1, has_side_effects=True, vmem_limit_bytes=56 * 1024 * 1024
         ),
     )(
         meta,
@@ -304,6 +814,16 @@
         s_vals.reshape(16, B, B),
     )
     return p1, q.reshape(ROWS, 1, B, B)
+
+
+def body(*args):
+    p1, q, flag = fast(*args)
+    return lax.cond(
+        flag[0, 0] > 0.5,
+        lambda p1, q, *args: dense(*args),
+        lambda p1, q, *args: (p1, q),
+        p1, q.reshape(ROWS, 1, B, B), *args,
+    )
 
 
 def solution(mesh):

time: 146 us -> 107 us (0.73)
  Pallas kernels: 138 us -> 102 us
  local copies, waits for them, and re-layouts: 6.73 us -> 3.38 us
    pallas_call x1, Pallas kernels: 138 us -> 102 us  [fast(): pl.pallas_call(fast_kernel, out_shape=(jax.ShapeDtypeStruct((ROWS, 2, B,...]
    unnamed x19 -> x18, local copies, waits for them, and re-layouts: 6.05 us -> 2.2 us
where the time goes in v2:
time: 107 us
  Pallas kernels  102 us (95%)
  local copies, waits for them, and re-layouts  3.38 us (3%)
  between operations  1.37 us (1%)
    pallas_call x1, Pallas kernels, fast(): pl.pallas_call(fast_kernel, out_shape=(jax.ShapeDtypeStruct((ROWS, 2, B,...  102 us
    unnamed x18, local copies, waits for them, and re-layouts  2.2 us

profile of v2, /device:TPU:1, one launch (start us, length us, event | category | flops | bytes accessed | tf_op | source)
XLA Modules:
  0.0 106.7 jit_solution(11175478361518272437)
XLA Ops:
  0.6 0.0 copy-start.7
  0.6 0.0 copy-start.4
  0.7 0.0 copy-start.5
  0.7 0.0 copy-start.3
  0.7 0.0 copy-start.6
  0.7 0.6 copy-done.7
  1.3 0.0 copy-done.4
  1.3 0.0 copy-done.5
  1.3 0.0 copy-done.3
  1.4 0.0 copy-done.6
  1.4 0.0 copy-start
  1.4 0.0 copy-start.1
  1.4 0.0 copy-start.2
  1.4 101.7 %shard_map.95 = (bf16[8,2,128,128]{3,2,1,0:T(8,128)(2,1)S(1)}, bf16[8,128,128]{2,1,0:T(8,128)(2,1)S(1)}, f32[8,128]{1,0:T(8,128)}) custom-call(s32[1,8]{1,0:T(1,128)S(1)} %bitcast.24, s32[2,8]{1,0:T(2,128)S(1)} %bitcast.21, s32[2,8]{1,0:T(2,128)S(1)} %bitcast.22, s32[2,8]{1,0:T(2,128)S(1)} %bitcast.23, s32[1,8]{1,0:T(1,128)S(1)} %bitcast.25, ...), custom_call_target="tpu_custom_call" | custom-call | tf_op jit(solution)/shard_map/pallas_call | solution.py:461
  103.1 1.2 %slice.3 = f32[1,1]{1,0:T(1,128)} slice(f32[8,128]{1,0:T(8,128)} %get-tuple-element.40), slice={[0:1], [0:1]} | slice | bytes 8 | tf_op jit(solution)/shard_map/slice | solution.py:822
  104.9 0.0 copy-done
  104.9 0.0 copy-done.1
  104.9 0.0 copy-done.2
  105.0 0.2 conditional.1
  105.2 0.8 copy.22
  106.0 0.7 copy.23
Async XLA Ops:
  0.6 0.7 copy-start.7
  0.6 0.7 copy-start.4
  0.7 0.7 copy-start.5
  0.7 0.7 copy-start.3
  0.7 0.7 copy-start.6
  1.4 103.6 %copy-start = (bf16[8,2,128,128]{3,2,1,0:T(8,128)(2,1)S(1)}, bf16[8,2,128,128]{3,2,1,0:T(8,128)(2,1)}, u32[]{:S(2)}) copy-start(bf16[8,2,128,128]{3,2,1,0:T(8,128)(2,1)} %param.12) | copy-start | bytes 1572868
  1.4 103.6 %copy-start.1 = (bf16[8,2,128,128]{3,2,1,0:T(8,128)(2,1)S(1)}, bf16[8,2,128,128]{3,2,1,0:T(8,128)(2,1)}, u32[]{:S(2)}) copy-start(bf16[8,2,128,128]{3,2,1,0:T(8,128)(2,1)} %param.14) | copy-start | bytes 1572868
  1.4 103.6 %copy-start.2 = (bf16[8,1,128,128]{3,2,1,0:T(8,128)(2,1)S(1)}, bf16[8,1,128,128]{3,2,1,0:T(8,128)(2,1)}, u32[]{:S(2)}) copy-start(bf16[8,1,128,128]{3,2,1,0:T(8,128)(2,1)} %param.10) | copy-start | bytes 786436

commit v3 on v2

--- a/solution.py
+++ b/solution.py
@@ -303,7 +303,6 @@
         return table
 
     found = own_code(0)
-    found_s = own_code(1)
     panel_round(0, 0)
     z_round(f1_all, 8, 4, f1_sems, 0)
     lists = [pltpu.make_async_copy(list_v.at[w], list_s.at[w], smem_sem.at[w]) for w in range(2)]
@@ -338,16 +337,17 @@
 
     pack(0, list_s.at[0])
     settle[0].start()
+    found_s = own_code(1)
     z_round(f1_all, 8, 4, f1_sems, 3)
     over = own_index(0, *found)
     first_index = pltpu.make_async_copy(index_v.at[0], index_s.at[0], smem_sem.at[2])
     first_index.start()
-    list_v[1] = peer_lists(1).astype(I32)
-    lists[1].start()
     z_round(f1_all, 8, 4, f1_sems, 4)
     relay(0)
     panel_begin(1)
     z_round(f1_all, 8, 4, f1_sems, 5)
+    list_v[1] = peer_lists(1).astype(I32)
+    lists[1].start()
     over = over + own_index(1, *found_s)
     second_index = pltpu.make_async_copy(index_v.at[1], index_s.at[1], smem_sem.at[3])
     second_index.start()
@@ -391,13 +391,15 @@
         part_send_row(2 * h + 1)
         if h > 0:
             finish(h - 1)
+        if h == 2:
+            panel_round(1, 0)
     finish(3)
 
     for step in range(1, TILES):
         send(flag_own.at[0], flag_row.at[step - 1], flag_send.at[step - 1], flag_recv.at[step - 1], row_peer(step))
     z_round(p1_all, 16, 4, p1_sems, 0)
-    for n in range(3):
-        panel_round(1, n)
+    panel_round(1, 1)
+    panel_round(1, 2)
     pack(1, list_s.at[1])
     settle[1].start()
     z_round(p1_all, 16, 4, p1_sems, 1)
@@ -421,9 +423,8 @@
     send(flag_own.at[2], flag_core, flag_send.at[at], flag_recv.at[at], core_peer)
     z_round(p1_all, 16, 4, p1_sems, 4)
     arrived(flag_core, flag_send.at[at], flag_recv.at[at], core_peer)
-    total = jnp.sum(total + flag_core[...], axis=0, keepdims=True)
-    total = jnp.sum(total, axis=1, keepdims=True)
-    flag_ref[...] = jnp.broadcast_to(total, (8, B))
+    total = total + flag_core[...]
+    flag_ref[0, 0] = jnp.where(jnp.sum(total) > 0.5, 1, 0)
     z_round(p1_all, 16, 4, p1_sems, 5)
     packets_arrived(1)
     settle[1].wait()
@@ -463,10 +464,10 @@
         out_shape=(
             jax.ShapeDtypeStruct((ROWS, 2, B, B), BF16),
             jax.ShapeDtypeStruct((ROWS, B, B), BF16),
-            jax.ShapeDtypeStruct((8, B), F32),
+            jax.ShapeDtypeStruct((1, 1), I32),
         ),
         in_specs=[vmem] * 5 + [pl.BlockSpec(memory_space=pl.ANY)] * 3,
-        out_specs=(vmem,) * 3,
+        out_specs=(vmem, vmem, pl.BlockSpec(memory_space=pltpu.SMEM)),
         scratch_shapes=[
             pltpu.VMEM((PACKED, B, B), BF16),
             pltpu.VMEM((PACKED, B, B), BF16),
@@ -819,7 +820,7 @@
 def body(*args):
     p1, q, flag = fast(*args)
     return lax.cond(
-        flag[0, 0] > 0.5,
+        flag[0, 0] > 0,
         lambda p1, q, *args: dense(*args),
         lambda p1, q, *args: (p1, q),
         p1, q.reshape(ROWS, 1, B, B), *args,

time: 107 us -> 102 us (0.953)
  Pallas kernels: 102 us -> 98.6 us
  local copies, waits for them, and re-layouts: 3.38 us -> 2.2 us
    pallas_call x1, Pallas kernels: 102 us -> 98.6 us  [fast(): pl.pallas_call(fast_kernel, out_shape=(jax.ShapeDtypeStruct((ROWS, 2, B,...]
    slice x1 -> x0, local copies, waits for them, and re-layouts: 1.18 us -> none  [body(): flag[0, 0] > 0.5]
where the time goes in v3:
time: 102 us
  Pallas kernels  98.6 us (97%)
  local copies, waits for them, and re-layouts  2.2 us (2%)
  between operations  1.36 us (1%)
    pallas_call x1, Pallas kernels, fast(): pl.pallas_call(fast_kernel, out_shape=(jax.ShapeDtypeStruct((ROWS, 2, B,...  98.6 us
    unnamed x18, local copies, waits for them, and re-layouts  2.2 us

profile of v3, /device:TPU:1, one launch (start us, length us, event | category | flops | bytes accessed | tf_op | source)
XLA Modules:
  0.0 102.3 jit_solution(7276869338034236804)
XLA Ops:
  0.6 0.0 copy-start.7
  0.6 0.0 copy-start.4
  0.7 0.0 copy-start.5
  0.7 0.0 copy-start.3
  0.7 0.0 copy-start.6
  0.7 0.6 copy-done.7
  1.3 0.0 copy-done.4
  1.3 0.0 copy-done.5
  1.3 0.0 copy-done.3
  1.4 0.0 copy-done.6
  1.4 0.0 copy-start
  1.4 0.0 copy-start.1
  1.4 0.0 copy-start.2
  1.4 98.6 %shard_map.95 = (bf16[8,2,128,128]{3,2,1,0:T(8,128)(2,1)S(1)}, bf16[8,128,128]{2,1,0:T(8,128)(2,1)S(1)}, s32[1,1]{1,0:T(1,128)}) custom-call(s32[1,8]{1,0:T(1,128)S(1)} %bitcast.24, s32[2,8]{1,0:T(2,128)S(1)} %bitcast.21, s32[2,8]{1,0:T(2,128)S(1)} %bitcast.22, s32[2,8]{1,0:T(2,128)S(1)} %bitcast.23, s32[1,8]{1,0:T(1,128)S(1)} %bitcast.25, ...), custom_call_target="tpu_custom_call" | custom-call | tf_op jit(solution)/shard_map/pallas_call | solution.py:462
  100.6 0.0 copy-done
  100.6 0.0 copy-done.1
  100.6 0.0 copy-done.2
  100.6 0.2 conditional.1
  100.8 0.8 copy.22
  101.6 0.7 copy.23
Async XLA Ops:
  0.6 0.7 copy-start.7
  0.6 0.7 copy-start.4
  0.7 0.7 copy-start.5
  0.7 0.7 copy-start.3
  0.7 0.7 copy-start.6
  1.4 99.2 %copy-start = (bf16[8,2,128,128]{3,2,1,0:T(8,128)(2,1)S(1)}, bf16[8,2,128,128]{3,2,1,0:T(8,128)(2,1)}, u32[]{:S(2)}) copy-start(bf16[8,2,128,128]{3,2,1,0:T(8,128)(2,1)} %param.12) | copy-start | bytes 1572868
  1.4 99.2 %copy-start.1 = (bf16[8,2,128,128]{3,2,1,0:T(8,128)(2,1)S(1)}, bf16[8,2,128,128]{3,2,1,0:T(8,128)(2,1)}, u32[]{:S(2)}) copy-start(bf16[8,2,128,128]{3,2,1,0:T(8,128)(2,1)} %param.14) | copy-start | bytes 1572868
  1.4 99.2 %copy-start.2 = (bf16[8,1,128,128]{3,2,1,0:T(8,128)(2,1)S(1)}, bf16[8,1,128,128]{3,2,1,0:T(8,128)(2,1)}, u32[]{:S(2)}) copy-start(bf16[8,1,128,128]{3,2,1,0:T(8,128)(2,1)} %param.10) | copy-start | bytes 786436

commit v4 on v3

--- a/solution.py
+++ b/solution.py
@@ -11,8 +11,8 @@
 NZ = 8
 ROWS = 8
 TILES = SIDE * SIDE
-CAP = 12
-HALF = CAP // 2
+CAP = 11
+HALF = 6
 PACKED = 65
 BLOCKS = PACKED + 6 * CAP
 F32, I32, BF16 = jnp.float32, jnp.int32, jnp.bfloat16
@@ -129,14 +129,17 @@
         return bufs[which].at[pl.ds(PACKED + (h * 3 + d - 1) * CAP, CAP)]
 
     def half_of(ref, e):
-        return ref.at[pl.ds(e * HALF, HALF)]
+        return ref.at[pl.ds(e * HALF, HALF if e == 0 else CAP - HALF)]
+
+    def relayed(which, h, e):
+        return relays.at[which, h, e, pl.ds(0, HALF if e == 0 else CAP - HALF)]
 
     def relay(which):
         for h in range(2):
             for e, way in ((0, 1), (1, -1)):
-                arrived(relays.at[which, h, e], rel_send.at[which, h, e], rel_recv.at[which, h, e], along(1 - h, way))
+                arrived(relayed(which, h, e), rel_send.at[which, h, e], rel_recv.at[which, h, e], along(1 - h, way))
                 send(
-                    relays.at[which, h, e], half_of(packet(which, h, 2), e),
+                    relayed(which, h, e), half_of(packet(which, h, 2), e),
                     pack_send.at[which, h, 3 + e], pack_recv.at[which, h, 3 + e], along(1 - h, way),
                 )
 
@@ -312,7 +315,6 @@
     panel_round(0, 1)
     panel_round(0, 2)
     settle = [pltpu.make_async_copy(whole[w], bufs[w].at[pl.ds(0, PACKED)], local_sem.at[5 + w]) for w in range(2)]
-    z_round(f1_all, 8, 4, f1_sems, 2)
     lists[0].wait()
 
     def pack(which, ref):
@@ -325,7 +327,7 @@
                 if d == 2:
                     for e, way in ((0, 1), (1, -1)):
                         send(
-                            half_of(outs.at[which, h, 1], e), relays.at[which, h, e],
+                            half_of(outs.at[which, h, 1], e), relayed(which, h, e),
                             rel_send.at[which, h, e], rel_recv.at[which, h, e], along(axis, way),
                         )
                 else:
@@ -337,6 +339,7 @@
 
     pack(0, list_s.at[0])
     settle[0].start()
+    z_round(f1_all, 8, 4, f1_sems, 2)
     found_s = own_code(1)
     z_round(f1_all, 8, 4, f1_sems, 3)
     over = own_index(0, *found)

time: 102 us -> 98.9 us (0.970)
  Pallas kernels: 98.6 us -> 95.1 us
    pallas_call x1, Pallas kernels: 98.6 us -> 95.1 us  [fast(): pl.pallas_call(fast_kernel, out_shape=(jax.ShapeDtypeStruct((ROWS, 2, B,...]
where the time goes in v4:
time: 98.9 us; the launch traced here: 98.8 us
  Pallas kernels  95.1 us (96%)
  local copies, waits for them, and re-layouts  2.2 us (2%)
  between operations  1.36 us (1%)
    pallas_call x1, Pallas kernels, fast(): pl.pallas_call(fast_kernel, out_shape=(jax.ShapeDtypeStruct((ROWS, 2, B,...  95.1 us
    unnamed x18, local copies, waits for them, and re-layouts  2.2 us

profile of v4, /device:TPU:1, one launch (start us, length us, event | category | flops | bytes accessed | tf_op | source)
XLA Modules:
  0.0 98.8 jit_solution(17929689025946762049)
XLA Ops:
  0.6 0.0 copy-start.7
  0.6 0.0 copy-start.4
  0.7 0.0 copy-start.5
  0.7 0.0 copy-start.3
  0.7 0.0 copy-start.6
  0.7 0.6 copy-done.7
  1.3 0.0 copy-done.4
  1.3 0.0 copy-done.5
  1.3 0.0 copy-done.3
  1.4 0.0 copy-done.6
  1.4 0.0 copy-start
  1.4 0.0 copy-start.1
  1.4 0.0 copy-start.2
  1.4 95.1 %shard_map.95 = (bf16[8,2,128,128]{3,2,1,0:T(8,128)(2,1)S(1)}, bf16[8,128,128]{2,1,0:T(8,128)(2,1)S(1)}, s32[1,1]{1,0:T(1,128)}) custom-call(s32[1,8]{1,0:T(1,128)S(1)} %bitcast.24, s32[2,8]{1,0:T(2,128)S(1)} %bitcast.21, s32[2,8]{1,0:T(2,128)S(1)} %bitcast.22, s32[2,8]{1,0:T(2,128)S(1)} %bitcast.23, s32[1,8]{1,0:T(1,128)S(1)} %bitcast.25, ...), custom_call_target="tpu_custom_call" | custom-call | tf_op jit(solution)/shard_map/pallas_call | solution.py:465
  97.1 0.0 copy-done
  97.1 0.0 copy-done.1
  97.1 0.0 copy-done.2
  97.1 0.2 conditional.1
  97.3 0.8 copy.22
  98.1 0.7 copy.23
Async XLA Ops:
  0.6 0.7 copy-start.7
  0.6 0.7 copy-start.4
  0.7 0.7 copy-start.5
  0.7 0.7 copy-start.3
  0.7 0.7 copy-start.6
  1.4 95.7 %copy-start = (bf16[8,2,128,128]{3,2,1,0:T(8,128)(2,1)S(1)}, bf16[8,2,128,128]{3,2,1,0:T(8,128)(2,1)}, u32[]{:S(2)}) copy-start(bf16[8,2,128,128]{3,2,1,0:T(8,128)(2,1)} %param.12) | copy-start | bytes 1572868
  1.4 95.8 %copy-start.1 = (bf16[8,2,128,128]{3,2,1,0:T(8,128)(2,1)S(1)}, bf16[8,2,128,128]{3,2,1,0:T(8,128)(2,1)}, u32[]{:S(2)}) copy-start(bf16[8,2,128,128]{3,2,1,0:T(8,128)(2,1)} %param.14) | copy-start | bytes 1572868
  1.4 95.8 %copy-start.2 = (bf16[8,1,128,128]{3,2,1,0:T(8,128)(2,1)S(1)}, bf16[8,1,128,128]{3,2,1,0:T(8,128)(2,1)}, u32[]{:S(2)}) copy-start(bf16[8,1,128,128]{3,2,1,0:T(8,128)(2,1)} %param.10) | copy-start | bytes 786436
